TPU v7x, 32 devices: a whole 2x2x4 slice. The times are simulated.
32 devices in a mesh: groups: 2 (over y), replica: 8 (over z, x), tensor: 2 (over core).
Axes of the slice: x: 2, y: 2, z: 4, core: 2. Of those that a mesh axis runs over, the one named last changes fastest.
Arguments:
- hidden: bfloat16 [4, 512, 8192], P(None, ('groups', 'replica'), 'tensor'), parts along dimension 1, may hold values from -6 to 6
- down_weight: bfloat16 [16, 64, 8192], P('replica', None, 'tensor'), may hold values from -0.0625 to 0.0625
- up_weight: bfloat16 [16, 64, 8192], P('replica', None, 'tensor'), may hold values from -0.75 to 0.75
- adapter_update_scale: float32 [16], replicated, may hold values from 0.5 to 2
- input_norm_weight: float32 [8192], P('tensor'), may hold values from 0.75 to 1.3
- segment_length: int32 [32], P('groups'), parts along dimension 0, may hold values from 8 to 16, as said below
- moves: int32 [8, 3], P('groups'), parts along dimension 0, may hold values from 0 to 7, as said below
Outputs:
- served: bfloat16 [4, 768, 8192], P(None, ('groups', 'replica'), 'tensor'), parts along dimension 1
There are 2 independent parts, one for each index of `groups`. A program takes and returns all parts, laid end to end along the dimension named above; an argument that names none is the same for every part. Nothing has to cross between parts.
Inputs may be any that keep to these rules, and one draw needn't show every extreme that they name: `moves`: column 0 names 4 different source replicas and column 2 names 4 different target replicas, none of which is a source; column 1 is below 2. `segment_length`: every segment named by moves has 16 live requests.
All inputs are finite; a program needn't handle non-finite values.
Results may differ from a plain program's by a relative error of at most 0.0057.
Values may be sent and summed in bfloat16 or wider, within the bound.
No kernel may reach another device: no remote copies, remote signals or barrier semaphores. Data moves between devices by JAX's collectives and lax.ppermute only.
A program may use at most 64 MiB of HBM per device.

v0:
```python
import jax
import jax.numpy as jnp
from jax import lax
from jax.sharding import PartitionSpec as P

MODEL_WIDTH = 8192
MOVES = 4


epsilon = 1e-05


def broadcast(block, axis, holder):
    block = jnp.where(lax.axis_index(axis) == holder, block, jnp.zeros_like(block))
    return lax.psum(block, axis)


def apply_lowrank_updates(request_rows, shrink_weights, expand_weights, scales, input_norm_weight):
    steps, count, segment, halved_width = request_rows.shape
    rank_extent = shrink_weights.shape[1]
    values = request_rows.astype(jnp.float32)
    squares = lax.psum(jnp.sum(values * values, axis=3), "tensor")
    normed = (
        values * lax.rsqrt(squares[:, :, :, None] / MODEL_WIDTH + epsilon) * input_norm_weight
    ).astype(jnp.bfloat16)
    partial_value = jnp.einsum(
        "tnsd,nrd->tnsr", normed, shrink_weights, preferred_element_type=jnp.float32
    )
    shrink = lax.psum(partial_value.reshape(steps * count, segment * rank_extent), "tensor")
    shrink = shrink.reshape(steps, count, segment, rank_extent).astype(jnp.bfloat16)
    delta = jnp.einsum("tnsr,nrd->tnsd", shrink, expand_weights, preferred_element_type=jnp.float32)
    return (delta * scales[None, :, None, None]).astype(jnp.bfloat16)


def on_device(
    hidden, down_weight, up_weight, adapter_update_scale, input_norm_weight, segment_length, moves
):
    local_adapter_count, rank_extent, halved_width = down_weight.shape
    steps = hidden.shape[0]
    segment = hidden.shape[1] // local_adapter_count
    self_index = lax.axis_index("replica")
    first_id = self_index * local_adapter_count
    lengths = lax.dynamic_slice_in_dim(segment_length, first_id, local_adapter_count)
    alive = jnp.arange(segment, dtype=jnp.int32)[None, :] < lengths[:, None]
    resident_rows = jnp.where(
        alive[None, :, :, None],
        hidden.reshape(steps, local_adapter_count, segment, halved_width),
        jnp.zeros((), jnp.bfloat16),
    )
    sources = moves[:, 0]
    slot_numbers = moves[:, 1]
    targets = moves[:, 2]
    leaving = sources == self_index
    sending = jnp.any(leaving)
    output_position = jnp.sum(jnp.where(leaving, slot_numbers, 0))
    leaving_rows = lax.dynamic_index_in_dim(resident_rows, output_position, 1, keepdims=False)
    parcel = jnp.concatenate(
        [
            lax.dynamic_index_in_dim(down_weight, output_position, 0, keepdims=False),
            lax.dynamic_index_in_dim(up_weight, output_position, 0, keepdims=False),
            leaving_rows.reshape(steps * segment, halved_width),
        ],
        axis=0,
    )
    parcel = jnp.where(sending, parcel, jnp.zeros_like(parcel))
    removed = jnp.logical_and(
        jnp.arange(local_adapter_count, dtype=jnp.int32) == output_position, sending
    )
    arriving = targets == self_index
    guest_adapter = jnp.sum(jnp.where(arriving, sources * local_adapter_count + slot_numbers, 0))
    guest = jnp.zeros_like(parcel)
    for move in range(MOVES):
        arrived = broadcast(parcel, "replica", sources[move])
        guest = jnp.where(targets[move] == self_index, arrived, guest)
    visiting_reduction = guest[:rank_extent]
    visiting_expansion = guest[rank_extent : 2 * rank_extent]
    guest_rows = guest[2 * rank_extent :].reshape(steps, 1, segment, halved_width)
    kept_rows = jnp.where(
        removed[None, :, None, None], jnp.zeros_like(resident_rows), resident_rows
    )
    resident_scale = lax.dynamic_slice_in_dim(adapter_update_scale, first_id, local_adapter_count)
    guest_scale = lax.dynamic_slice_in_dim(adapter_update_scale, guest_adapter, 1)
    result = apply_lowrank_updates(
        jnp.concatenate([kept_rows, guest_rows], axis=1),
        jnp.concatenate([down_weight, visiting_reduction[None]], axis=0),
        jnp.concatenate([up_weight, visiting_expansion[None]], axis=0),
        jnp.concatenate([resident_scale, guest_scale], axis=0),
        input_norm_weight,
    )
    return result.reshape(steps, (local_adapter_count + 1) * segment, halved_width)


def solution(mesh):
    return jax.shard_map(
        on_device,
        mesh=mesh,
        in_specs=(
            P(None, ("groups", "replica"), "tensor"),
            P("replica", None, "tensor"),
            P("replica", None, "tensor"),
            P(),
            P("tensor"),
            P("groups"),
            P("groups", None),
        ),
        out_specs=P(None, ("groups", "replica"), "tensor"),
        check_vma=False,
    )
```

profile of v0, /device:TPU:0, one launch (start us, length us, event | category | flops | bytes accessed | tf_op | source)
XLA Modules:
  0.0 259.6 jit_solution(5114959483749417553)
XLA Ops:
  6.5 1.6 fusion.20
  8.2 1.3 fusion.19
  9.5 1.6 select_reduce_fusion
  12.3 0.7 dynamic_slice.22
  13.0 0.1 iota_compare_fusion
  13.1 1.2 compare_and_fusion
  17.5 1.6 broadcast_select_fusion.4
  19.1 0.2 copy-done.1
  19.3 0.1 dynamic-slice_bitcast_fusion
  19.4 4.1 %broadcast_select_fusion = (bf16[192,4096]{1,0:T(8,128)(2,1)}, bf16[192,4096]{1,0:T(8,128)(2,1)}, bf16[192,4096]{1,0:T(8,128)(2,1)}, bf16[192,4096]{1,0:T(8,128)(2,1)}) fusion(pred[]{:T(512)S(6)} %eq.55, bf16[64,4096]{1,0:T(8,128)(2,1)S(1)} %bitcast.38, bf16[64,4096]{1,0:T(8,128)(2,1)S(1)} %get-tuple-element.30, bf16[64,4096]{1,0:T(8,128)(2,1)S(1)} %get-tuple-element.31, ...), kind=kLoop, calls=%fused_computation.20 | loop fusion | flops 8650752 | bytes 7864325 | tf_op jit(solution)/shard_map/jit(_where)/select_n | solution.py:14
  24.8 0.1 dynamic_slice.24
  25.5 0.6 dynamic_slice.25
  28.5 0.7 pad_maximum_fusion.2
  29.2 211.5 %all-reduce.3.cloned.1.call-done = (bf16[192,4096]{1,0:T(8,128)(2,1)}, bf16[192,4096]{1,0:T(8,128)(2,1)}, bf16[192,4096]{1,0:T(8,128)(2,1)}, bf16[192,4096]{1,0:T(8,128)(2,1)}) async-done(((bf16[192,4096]{1,0:T(8,128)(2,1)}, bf16[192,4096]{1,0:T(8,128)(2,1)}, bf16[192,4096]{1,0:T(8,128)(2,1)}, bf16[192,4096]{1,0:T(8,128)(2,1)}), (bf16[192,4096]{1,0:T(8,128)(2,1)}, bf16[192,4096]{1,0:T(8,128)(2,1)}, ...) | async-done | bytes 6291472 | tf_op jit(solution)/shard_map/psum | solution.py:15
  240.7 0.3 select_select_fusion
  241.0 0.1 slice_bitcast_fusion
  241.1 0.4 fusion.2
  241.5 2.5 psum.46
  244.0 1.9 fusion.13
  245.9 0.1 reshape.80
  246.0 3.6 %psum.47 = bf16[12,1024]{1,0:T(8,128)(2,1)S(1)} all-reduce(f32[12,1024]{1,0:T(8,128)S(1)} %reshape.80), channel_id=1, replica_groups=mesh['groups'=2,'replica'=8,'tensor'=2] {'tensor'}, use_global_device_ids=true, to_apply=%region_8.9 | all-reduce | flops 12288 | bytes 73728 | tf_op jit(solution)/shard_map/psum | solution.py:29
  249.6 0.1 convert_element_type.21
  249.7 1.8 fusion.1
  251.5 1.2 copy.12
  (12 shorter events, 0.1 us)
Async XLA Ops:
  6.5 234.2 %all-reduce.3.cloned.1.call-start = ((), (), s32[]{:S(2)}) async-start(), calls=%async_computation | async-start | bytes 12582912 | tf_op jit(solution)/shard_map/psum | solution.py:15
  17.5 1.7 copy-start
  17.5 1.8 copy-start.1
  23.5 1.3 copy-start.3
  241.1 2.9 %copy-start.2 = (f32[4096]{0:T(1024)S(1)}, f32[4096]{0:T(1024)}, u32[]{:S(2)}) copy-start(f32[4096]{0:T(1024)} %param.11) | copy-start | bytes 49156
Sparse Core Ops, SparseCore 0:
  23.6 217.0 all-reduce.2
where the time goes:
time: 260 us
  waiting for transfers between devices  211 us (81%)
  between operations  22.3 us (9%)
  other arithmetic  11.1 us (4%)
  blocking collectives  6.1 us (2%)
  local copies, waits for them, and re-layouts  4.95 us (2%)
  matrix products  3.69 us (1%)
    psum x1, waiting for transfers between devices, broadcast(): return lax.psum(block, axis)  211 us
  transfers between devices with their start and end apart: 1, of which 1 were waited for; matrix products, arithmetic and copies ran while one was open for 1% of the time, Pallas kernels for 0%

commit v1 on v0

v1 whole, which is shorter than its diff:
```python
import functools

import jax
import jax.numpy as jnp
from jax import lax
from jax.experimental import pallas as pl
from jax.experimental.pallas import tpu as pltpu
from jax.sharding import PartitionSpec as P

MODEL_WIDTH = 8192
MOVES = 4
EPSILON = 1e-05
ROW_BLOCK = 16
VMEM_LIMIT = 48 * 1024 * 1024

SMEM = pl.BlockSpec(memory_space=pltpu.SMEM)
VMEM = pl.BlockSpec(memory_space=pltpu.VMEM)
ANY = pl.BlockSpec(memory_space=pl.ANY)
F32 = jnp.float32
BF16 = jnp.bfloat16


def params():
    return pltpu.CompilerParams(vmem_limit_bytes=VMEM_LIMIT)


def leaving_slot(moves, me):
    slot, sending = jnp.int32(0), jnp.int32(0)
    for move in range(MOVES):
        here = moves[move, 0] == me
        slot = jnp.where(here, moves[move, 1], slot)
        sending = jnp.where(here, 1, sending)
    return slot, sending


def source_of(moves, target, otherwise):
    source = otherwise
    for move in range(MOVES):
        source = jnp.where(moves[move, 2] == target, moves[move, 0], source)
    return source


def piece_place(index, blocks):
    return index % blocks, index // blocks


def cut_kernel(pieces, width, me_ref, moves, up, *refs):
    outs, sems = refs[:pieces], refs[pieces]
    slot, _ = leaving_slot(moves, me_ref[0])
    blocks = up.shape[1] // ROW_BLOCK
    copies = []
    for index in range(pieces):
        rows, columns = piece_place(index, blocks)
        copies.append(
            pltpu.make_async_copy(
                up.at[slot, pl.ds(rows * ROW_BLOCK, ROW_BLOCK), pl.ds(columns * width, width)],
                outs[index],
                sems.at[index],
            )
        )
    for copy in copies:
        copy.start()
    for copy in copies:
        copy.wait()


def project_kernel(hidden, down, gain, out):
    adapters, rank, width = down.shape
    steps = hidden.shape[0]
    chunk = 512
    for n in range(adapters):
        total = jnp.zeros((steps * ROW_BLOCK, rank), F32)
        squares = jnp.zeros((steps * ROW_BLOCK, 1), F32)
        for c in range(0, width, chunk):
            values = hidden[:, n * ROW_BLOCK : (n + 1) * ROW_BLOCK, c : c + chunk]
            values = values.reshape(steps * ROW_BLOCK, chunk).astype(F32)
            squares += jnp.sum(values * values, axis=1, keepdims=True)
            gained = values * gain[:, c : c + chunk]
            high = gained.astype(BF16)
            low = (gained - high.astype(F32)).astype(BF16)
            weights = down[n, :, c : c + chunk]
            for part in (high, low):
                total += lax.dot_general(
                    part, weights, (((1,), (1,)), ((), ())), preferred_element_type=F32
                )
        out[n] = jnp.concatenate(
            [total, jnp.broadcast_to(squares, (steps * ROW_BLOCK, rank))], axis=1
        )


def shrink_kernel(rank, me_ref, moves, lengths, mine, other, kept, rider):
    me = me_ref[0]
    slot, sending = leaving_slot(moves, me)
    adapters, rows, _ = mine.shape
    leaving = None
    for n in range(adapters):
        total = mine[n] + other[n]
        squares = total[:, rank : rank + 1]
        shrink = total[:, :rank] * lax.rsqrt(squares / MODEL_WIDTH + EPSILON)
        place = lax.broadcasted_iota(jnp.int32, (rows, rank), 0) % ROW_BLOCK
        shrink = jnp.where(place < lengths[me * adapters + n], shrink, 0.0)
        leaving = shrink if n == 0 else jnp.where(slot == n, shrink, leaving)
        removed = (sending == 1) & (slot == n)
        kept[n] = jnp.where(removed, 0.0, shrink).astype(BF16)
    leaving = leaving.astype(BF16)
    for t in range(rows // ROW_BLOCK):
        rider[:, t * rank : (t + 1) * rank] = leaving[t * ROW_BLOCK : (t + 1) * ROW_BLOCK]


def resident_kernel(me_ref, scales, kept, up, out, held, sem):
    adapters, rank, width = up.shape
    steps = held.shape[0]
    chunk = 1024
    for n in range(adapters):
        scale = scales[me_ref[0] * adapters + n]
        for c in range(0, width, chunk):
            delta = jnp.dot(kept[n], up[n, :, c : c + chunk], preferred_element_type=F32)
            held[:, n * ROW_BLOCK : (n + 1) * ROW_BLOCK, c : c + chunk] = (
                (delta * scale).astype(BF16).reshape(steps, ROW_BLOCK, chunk)
            )
    copy = pltpu.make_async_copy(held, out.at[:, : adapters * ROW_BLOCK, :], sem)
    copy.start()
    copy.wait()


def regroup_kernel(pieces, width, me_ref, moves, rider, *refs):
    arrived, outs = refs[:pieces], refs[pieces : 2 * pieces]
    held, sems = refs[2 * pieces :]
    me = me_ref[0]
    copies = [
        pltpu.make_async_copy(arrived[m], held.at[m], sems.at[m]) for m in range(pieces)
    ]
    for copy in copies:
        copy.start()
    for m in range(pieces):
        outs[m][:, width:] = rider[...]
    for copy in copies:
        copy.wait()
    for m in range(pieces):
        target = me ^ m
        outs[m][:, :width] = held[source_of(moves, target, target) ^ me]


def guest_kernel(pieces, width, me_ref, moves, scales, *refs):
    arrived = refs[:pieces]
    out = refs[pieces + 1]
    weights, rider, held, sems, rider_sem = refs[pieces + 2 :]
    me = me_ref[0]
    rank, full = weights.shape
    steps = held.shape[0]
    adapters = out.shape[1] // ROW_BLOCK - 1
    source = source_of(moves, me, me)
    visited = source != me
    slot, _ = leaving_slot(moves, source)
    scale = scales[source * adapters + slot]
    blocks = rank // ROW_BLOCK
    copies = []
    for m in range(pieces):
        rows, columns = piece_place(source ^ me ^ m, blocks)
        copies.append(
            pltpu.make_async_copy(
                arrived[m].at[:, pl.ds(0, width)],
                weights.at[
                    pl.ds(pl.multiple_of(rows * ROW_BLOCK, ROW_BLOCK), ROW_BLOCK),
                    pl.ds(pl.multiple_of(columns * width, 128), width),
                ],
                sems.at[m],
            )
        )
    for copy in copies:
        copy.start()
    size = rider.shape[1]
    for m in range(pieces):

        @pl.when((source ^ me) == m)
        def _():
            copy = pltpu.make_async_copy(
                arrived[m].at[:, pl.ds(width, size)], rider, rider_sem
            )
            copy.start()
            copy.wait()

    for copy in copies:
        copy.wait()
    shrink = jnp.concatenate(
        [rider[:, t * rank : (t + 1) * rank] for t in range(steps)], axis=0
    )
    chunk = 1024
    for c in range(0, full, chunk):
        delta = jnp.dot(shrink, weights[:, c : c + chunk], preferred_element_type=F32)
        delta = jnp.where(visited, delta * scale, 0.0)
        held[:, :, c : c + chunk] = delta.astype(BF16).reshape(steps, ROW_BLOCK, chunk)
    copy = pltpu.make_async_copy(
        held, out.at[:, pl.ds(adapters * ROW_BLOCK, ROW_BLOCK), :], rider_sem
    )
    copy.start()
    copy.wait()


def exchange(parts, replicas):
    done = [parts[0]] + [None] * (replicas - 1)
    for m in sorted(range(1, replicas), reverse=True):
        done[m] = lax.ppermute(parts[m], "replica", [(i, i ^ m) for i in range(replicas)])
    return done


def scattered(
    replicas, hidden, down_weight, up_weight, scales, gain, lengths, moves
):
    adapters, rank, width = down_weight.shape
    steps = hidden.shape[0]
    rows = steps * ROW_BLOCK
    piece = rank * width // (replicas * ROW_BLOCK)
    ride = rank * steps
    me = lax.axis_index("replica").astype(jnp.int32).reshape(1)
    shape = jax.ShapeDtypeStruct

    parts = pl.pallas_call(
        functools.partial(cut_kernel, replicas, piece),
        out_shape=[shape((ROW_BLOCK, piece), BF16)] * replicas,
        in_specs=[SMEM, SMEM, ANY],
        out_specs=[ANY] * replicas,
        scratch_shapes=[pltpu.SemaphoreType.DMA((replicas,))],
        compiler_params=params(),
        cost_estimate=pl.CostEstimate(
            flops=0, bytes_accessed=2 * rank * width * 2, transcendentals=0
        ),
        name="cut",
    )(me, moves, up_weight)
    parts = exchange(parts, replicas)

    mine = pl.pallas_call(
        project_kernel,
        out_shape=shape((adapters, rows, 2 * rank), F32),
        in_specs=[VMEM] * 3,
        out_specs=VMEM,
        compiler_params=params(),
        cost_estimate=pl.CostEstimate(
            flops=4 * adapters * rows * rank * width,
            bytes_accessed=4 * adapters * rows * width,
            transcendentals=0,
        ),
        name="project",
    )(hidden, down_weight, gain.reshape(1, width))
    other = lax.ppermute(mine, "tensor", [(0, 1), (1, 0)])
    kept, rider = pl.pallas_call(
        functools.partial(shrink_kernel, rank),
        out_shape=[shape((adapters, rows, rank), BF16), shape((ROW_BLOCK, ride), BF16)],
        in_specs=[SMEM, SMEM, SMEM, VMEM, VMEM],
        out_specs=[VMEM, VMEM],
        compiler_params=params(),
        name="shrink",
    )(me, moves, lengths, mine, other)
    out_shape = shape((steps, (adapters + 1) * ROW_BLOCK, width), BF16)
    out = pl.pallas_call(
        resident_kernel,
        out_shape=out_shape,
        in_specs=[SMEM, SMEM, VMEM, VMEM],
        out_specs=ANY,
        scratch_shapes=[
            pltpu.VMEM((steps, adapters * ROW_BLOCK, width), BF16),
            pltpu.SemaphoreType.DMA,
        ],
        compiler_params=params(),
        cost_estimate=pl.CostEstimate(
            flops=2 * adapters * rows * rank * width,
            bytes_accessed=4 * adapters * rows * width,
            transcendentals=0,
        ),
        name="resident",
    )(me, scales, kept, up_weight)

    parts = pl.pallas_call(
        functools.partial(regroup_kernel, replicas, piece),
        out_shape=[shape((ROW_BLOCK, piece + ride), BF16)] * replicas,
        in_specs=[SMEM, SMEM, VMEM] + [ANY] * replicas,
        out_specs=[VMEM] * replicas,
        scratch_shapes=[
            pltpu.VMEM((replicas, ROW_BLOCK, piece), BF16),
            pltpu.SemaphoreType.DMA((replicas,)),
        ],
        compiler_params=params(),
        cost_estimate=pl.CostEstimate(
            flops=0, bytes_accessed=2 * rank * width * 2, transcendentals=0
        ),
        name="regroup",
    )(me, moves, rider, *parts)
    parts = exchange(parts, replicas)

    return pl.pallas_call(
        functools.partial(guest_kernel, replicas, piece),
        out_shape=out_shape,
        in_specs=[SMEM, SMEM, SMEM] + [ANY] * (replicas + 1),
        out_specs=ANY,
        scratch_shapes=[
            pltpu.VMEM((rank, width), BF16),
            pltpu.VMEM((ROW_BLOCK, ride), BF16),
            pltpu.VMEM((steps, ROW_BLOCK, width), BF16),
            pltpu.SemaphoreType.DMA((replicas,)),
            pltpu.SemaphoreType.DMA,
        ],
        input_output_aliases={3 + replicas: 0},
        compiler_params=params(),
        cost_estimate=pl.CostEstimate(
            flops=2 * rows * rank * width,
            bytes_accessed=2 * (rank + rows) * width,
            transcendentals=0,
        ),
        name="guest",
    )(me, moves, scales, *parts, out)


def summed(hidden, down_weight, up_weight, scales, gain, lengths, moves):
    adapters, rank, width = down_weight.shape
    steps = hidden.shape[0]
    segment = hidden.shape[1] // adapters
    me = lax.axis_index("replica")
    first = me * adapters
    sources, slots, targets = moves[:, 0], moves[:, 1], moves[:, 2]
    here = lax.dynamic_slice_in_dim(lengths, first, adapters)
    alive = jnp.arange(segment, dtype=jnp.int32)[None, :] < here[:, None]
    values = jnp.where(
        alive[None, :, :, None], hidden.reshape(steps, adapters, segment, width), 0
    ).astype(F32)
    squares = lax.psum(jnp.sum(values * values, axis=3), "tensor")
    normed = (values * lax.rsqrt(squares[..., None] / MODEL_WIDTH + EPSILON) * gain).astype(BF16)
    shrink = jnp.einsum("tnsd,nrd->tnsr", normed, down_weight, preferred_element_type=F32)
    shrink = lax.psum(shrink, "tensor").astype(BF16)
    delta = jnp.einsum("tnsr,nrd->tnsd", shrink, up_weight, preferred_element_type=F32)
    scale = lax.dynamic_slice_in_dim(scales, first, adapters)
    served = (delta * scale[None, :, None, None]).astype(BF16)
    leaving = sources == me
    slot = jnp.sum(jnp.where(leaving, slots, 0))
    parcel = lax.dynamic_index_in_dim(served, slot, 1, keepdims=False)
    guest = jnp.zeros_like(parcel)
    for move in range(MOVES):
        arrived = lax.psum(jnp.where(leaving[move], parcel, jnp.zeros_like(parcel)), "replica")
        guest = jnp.where(targets[move] == me, arrived, guest)
    removed = (jnp.arange(adapters) == slot) & jnp.any(leaving)
    served = jnp.where(removed[None, :, None, None], jnp.zeros_like(served), served)
    result = jnp.concatenate([served, guest[:, None]], axis=1)
    return result.reshape(steps, (adapters + 1) * segment, width)


def solution(mesh):
    replicas = mesh.shape["replica"]
    body = functools.partial(scattered, replicas) if replicas == 8 else summed
    return jax.shard_map(
        body,
        mesh=mesh,
        in_specs=(
            P(None, ("groups", "replica"), "tensor"),
            P("replica", None, "tensor"),
            P("replica", None, "tensor"),
            P(),
            P("tensor"),
            P("groups"),
            P("groups", None),
        ),
        out_specs=P(None, ("groups", "replica"), "tensor"),
        check_vma=False,
    )
```

time: 260 us -> 46.6 us (0.18)
  waiting for transfers between devices: 211 us -> 10.6 us
  starting transfers between devices: 0.01 us -> 24.2 us
  between operations: 22.3 us -> 0.07 us
  other arithmetic: 11.1 us -> 0 us
  Pallas kernels: 0 us -> 8.13 us
  blocking collectives: 6.1 us -> 0 us
  matrix products: 3.69 us -> 0 us
    psum x1 -> x0, waiting for transfers between devices: 211 us -> none  [broadcast(): return lax.psum(block, axis)]
    ppermute x0 -> x15, starting transfers between devices: none -> 24.2 us  [the longest x14 23.7 us: exchange(): lax.ppermute(parts[m], 'replica', [(i, i ^ m) for i in range(replicas)])]
    ppermute x0 -> x15, waiting for transfers between devices: none -> 10.6 us  [the longest x14 10.6 us: exchange(): lax.ppermute(parts[m], 'replica', [(i, i ^ m) for i in range(replicas)])]
    pallas_call x0 -> x6, Pallas kernels: none -> 8.13 us  [the longest x1 2.32 us: scattered(): pl.pallas_call(functools.partial(guest_kernel, replicas, piece), out_shap...]
    psum x2 -> x0, blocking collectives: 6.1 us -> none  [the longest x1 3.62 us: apply_lowrank_updates(): lax.psum(partial_value.reshape(steps * count, segment * rank_extent), 'te...]
    select_n x3 -> x0, other arithmetic: 5.93 us -> none  [the longest x1 4.07 us: broadcast(): jnp.where(lax.axis_index(axis) == holder, block, jnp.zeros_like(block))]
    dot_general x2 -> x0, matrix products: 3.69 us -> none  [the longest x1 1.9 us: apply_lowrank_updates(): jnp.einsum('tnsd,nrd->tnsr', normed, shrink_weights, preferred_element_ty...]
    unnamed x8 -> x14, local copies, waits for them, and re-layouts: 0.21 us -> 3.27 us
  transfers between devices with their start and end apart: 1 -> 15, of which waited for: 1 -> 4; matrix products, arithmetic and copies ran while one was open for 1% -> 0% of each run, Pallas kernels for 0% -> 8%
where the time goes in v1:
time: 46.6 us; the launch traced here: 46.3 us
  starting transfers between devices  24.2 us (52%)
  waiting for transfers between devices  10.6 us (23%)
  Pallas kernels  8.13 us (17%)
  local copies, waits for them, and re-layouts  3.27 us (7%)
    ppermute x14, starting transfers between devices, exchange(): lax.ppermute(parts[m], 'replica', [(i, i ^ m) for i in range(replicas)])  23.7 us
    ppermute x14, waiting for transfers between devices, exchange(): lax.ppermute(parts[m], 'replica', [(i, i ^ m) for i in range(replicas)])  10.6 us
    unnamed x14, local copies, waits for them, and re-layouts  3.27 us
    pallas_call x1, Pallas kernels, scattered(): pl.pallas_call(functools.partial(guest_kernel, replicas, piece), out_shap...  2.32 us
    pallas_call x1, Pallas kernels, scattered(): pl.pallas_call(resident_kernel, out_shape=out_shape, in_specs=[SMEM, SMEM...  1.94 us
    pallas_call x1, Pallas kernels, scattered(): pl.pallas_call(functools.partial(regroup_kernel, replicas, piece), out_sh...  1.37 us
    pallas_call x1, Pallas kernels, scattered(): pl.pallas_call(functools.partial(cut_kernel, replicas, piece), out_shape=...  1 us
  transfers between devices with their start and end apart: 15, of which 4 were waited for; matrix products, arithmetic and copies ran while one was open for 0% of the time, Pallas kernels for 8%

profile of v1, /device:TPU:0, one launch (start us, length us, event | category | flops | bytes accessed | tf_op | source)
XLA Modules:
  0.0 46.3 jit_solution(7240567619997663255)
XLA Ops:
  0.0 1.3 %copy-done.1 = bf16[4,32,4096]{2,1,0:T(8,128)(2,1)S(1)} copy-done((bf16[4,32,4096]{2,1,0:T(8,128)(2,1)S(1)}, bf16[4,32,4096]{2,1,0:T(8,128)(2,1)}, u32[]{:S(2)}) %copy-start.1) | copy-done | bytes 1048600
  1.3 1.2 %copy-done.2 = bf16[2,64,4096]{2,1,0:T(8,128)(2,1)S(1)} copy-done((bf16[2,64,4096]{2,1,0:T(8,128)(2,1)S(1)}, bf16[2,64,4096]{2,1,0:T(8,128)(2,1)}, u32[]{:S(2)}) %copy-start.2) | copy-done | bytes 1048600
  2.5 0.7 %copy-done.4 = f32[4096]{0:T(1024)S(1)} copy-done((f32[4096]{0:T(1024)S(1)}, f32[4096]{0:T(1024)}, u32[]{:S(2)}) %copy-start.4) | copy-done | bytes 16408
  3.3 0.8 %project.1.mine = f32[2,64,128]{2,1,0:T(8,128)S(1)} custom-call(bf16[4,32,4096]{2,1,0:T(8,128)(2,1)S(1)} %copy-done.1, bf16[2,64,4096]{2,1,0:T(8,128)(2,1)S(1)} %copy-done.2, f32[1,4096]{1,0:T(1,128)S(1)} %bitcast.2), custom_call_target="tpu_custom_call" | custom-call | flops 134217728 | bytes 2097152 | tf_op jit(solution)/shard_map/project/pallas_call | solution.py:232
  4.1 0.5 %collective-permute-start = (f32[2,64,128]{2,1,0:T(8,128)S(1)}, f32[2,64,128]{2,1,0:T(8,128)S(1)}, u32[]{:S(2)}, u32[]{:S(2)}) collective-permute-start(f32[2,64,128]{2,1,0:T(8,128)S(1)} %project.1.mine), channel_id=1, source_target_pairs={{0,1},{1,0},{2,3},{3,2},{4,5},{5,4},{6,7},{7,6},{8,9},{9,8},{10,11... | collective-permute-start | bytes 196616 | tf_op jit(solution)/shard_map/ppermute | solution.py:245
  4.6 1.0 %cut.1 = (bf16[16,2048]{1,0:T(8,128)(2,1)S(1)}, bf16[16,2048]{1,0:T(8,128)(2,1)S(1)}, bf16[16,2048]{1,0:T(8,128)(2,1)S(1)}, bf16[16,2048]{1,0:T(8,128)(2,1)S(1)}...) custom-call(s32[1]{0:T(128)} %bitcast.me_ref, ...), custom_call_target="tpu_custom_call" | custom-call | bytes 1048576 | tf_op jit(solution)/shard_map/cut/pallas_call | solution.py:218
  5.6 2.6 %collective-permute-start.1 = (bf16[16,2048]{1,0:T(8,128)(2,1)S(1)}, bf16[16,2048]{1,0:T(8,128)(2,1)S(1)}, u32[]{:S(2)}, u32[]{:S(2)}) collective-permute-start(bf16[16,2048]{1,0:T(8,128)(2,1)S(1)} %get-tuple-element.25), channel_id=1, source_target_pairs={{0,2},{2,0},{4,6},{6,4},{8,10},{10,8},{12,14},{14,12},{1,3},{3,1},... | collective-permute-start | bytes 196616 | tf_op jit(solution)/shard_map/ppermute | solution.py:203
  8.2 1.6 %collective-permute-start.2 = (bf16[16,2048]{1,0:T(8,128)(2,1)S(1)}, bf16[16,2048]{1,0:T(8,128)(2,1)S(1)}, u32[]{:S(2)}, u32[]{:S(2)}) collective-permute-start(bf16[16,2048]{1,0:T(8,128)(2,1)S(1)} %get-tuple-element.26), channel_id=1, source_target_pairs={{0,4},{2,6},{4,0},{6,2},{8,12},{10,14},{12,8},{14,10},{1,5},{3,7},... | collective-permute-start | bytes 196616 | tf_op jit(solution)/shard_map/ppermute | solution.py:203
  9.8 3.0 %collective-permute-start.4 = (bf16[16,2048]{1,0:T(8,128)(2,1)S(1)}, bf16[16,2048]{1,0:T(8,128)(2,1)S(1)}, u32[]{:S(2)}, u32[]{:S(2)}) collective-permute-start(bf16[16,2048]{1,0:T(8,128)(2,1)S(1)} %get-tuple-element.28), channel_id=1, source_target_pairs={{0,8},{2,10},{4,12},{6,14},{8,0},{10,2},{12,4},{14,6},{1,9},{3,11}... | collective-permute-start | bytes 196616 | tf_op jit(solution)/shard_map/ppermute | solution.py:203
  12.8 1.3 %collective-permute-start.5 = (bf16[16,2048]{1,0:T(8,128)(2,1)S(1)}, bf16[16,2048]{1,0:T(8,128)(2,1)S(1)}, u32[]{:S(2)}, u32[]{:S(2)}) collective-permute-start(bf16[16,2048]{1,0:T(8,128)(2,1)S(1)} %get-tuple-element.29), channel_id=1, source_target_pairs={{0,10},{2,8},{4,14},{6,12},{8,2},{10,0},{12,6},{14,4},{1,11},{3,9}... | collective-permute-start | bytes 196616 | tf_op jit(solution)/shard_map/ppermute | solution.py:203
  14.0 3.6 %collective-permute-start.6 = (bf16[16,2048]{1,0:T(8,128)(2,1)S(1)}, bf16[16,2048]{1,0:T(8,128)(2,1)S(1)}, u32[]{:S(2)}, u32[]{:S(2)}) collective-permute-start(bf16[16,2048]{1,0:T(8,128)(2,1)S(1)} %get-tuple-element.30), channel_id=1, source_target_pairs={{0,12},{2,14},{4,8},{6,10},{8,4},{10,6},{12,0},{14,2},{1,13},{3,15... | collective-permute-start | bytes 196616 | tf_op jit(solution)/shard_map/ppermute | solution.py:203
  17.7 0.7 %shrink.1 = (bf16[2,64,64]{2,1,0:T(8,128)(2,1)S(1)}, bf16[16,256]{1,0:T(8,128)(2,1)S(1)}) custom-call(s32[1]{0:T(128)} %bitcast.me_ref, s32[4,3]{1,0:T(4,128)S(1)} %copy-done.3, s32[16]{0:T(128)S(1)} %copy-done.6, f32[2,64,128]{2,1,0:T(8,128)S(1)} %project.1.mine, f32[2,64,128]{2,1,0:T(8,128)S(1)} %collective-permute-done.other), custom_call_target="tpu_custom_call" | custom-call | tf_op jit(solution)/shard_map/shrink/pallas_call | solution.py:246
  18.4 4.5 %collective-permute-done.5.refs_5_ = bf16[16,2048]{1,0:T(8,128)(2,1)S(1)} collective-permute-done((bf16[16,2048]{1,0:T(8,128)(2,1)S(1)}, bf16[16,2048]{1,0:T(8,128)(2,1)S(1)}, u32[]{:S(2)}, u32[]{:S(2)}) %collective-permute-start.5) | collective-permute-done | bytes 65568 | tf_op jit(solution)/shard_map/ppermute | solution.py:203
  22.9 1.8 %collective-permute-done.7.refs_7_ = bf16[16,2048]{1,0:T(8,128)(2,1)S(1)} collective-permute-done((bf16[16,2048]{1,0:T(8,128)(2,1)S(1)}, bf16[16,2048]{1,0:T(8,128)(2,1)S(1)}, u32[]{:S(2)}, u32[]{:S(2)}) %collective-permute-start.7) | collective-permute-done | bytes 65568 | tf_op jit(solution)/shard_map/ppermute | solution.py:203
  24.7 1.4 %regroup.1 = (bf16[16,2304]{1,0:T(8,128)(2,1)S(1)}, bf16[16,2304]{1,0:T(8,128)(2,1)S(1)}, bf16[16,2304]{1,0:T(8,128)(2,1)S(1)}, bf16[16,2304]{1,0:T(8,128)(2,1)S...) custom-call(s32[1]{0:T(128)} %bitcast.me_ref, ...), custom_call_target="tpu_custom_call" | custom-call | bytes 1048576 | tf_op jit(solution)/shard_map/regroup/pallas_call | solution.py:273
  26.1 0.6 %collective-permute-start.8 = (bf16[16,2304]{1,0:T(8,128)(2,1)S(1)}, bf16[16,2304]{1,0:T(8,128)(2,1)S(1)}, u32[]{:S(2)}, u32[]{:S(2)}) collective-permute-start(bf16[16,2304]{1,0:T(8,128)(2,1)S(1)} %get-tuple-element.33), channel_id=1, source_target_pairs={{0,2},{2,0},{4,6},{6,4},{8,10},{10,8},{12,14},{14,12},{1,3},{3,1},... | collective-permute-start | bytes 221192 | tf_op jit(solution)/shard_map/ppermute | solution.py:203
  26.7 2.5 %collective-permute-start.9 = (bf16[16,2304]{1,0:T(8,128)(2,1)S(1)}, bf16[16,2304]{1,0:T(8,128)(2,1)S(1)}, u32[]{:S(2)}, u32[]{:S(2)}) collective-permute-start(bf16[16,2304]{1,0:T(8,128)(2,1)S(1)} %get-tuple-element.34), channel_id=1, source_target_pairs={{0,4},{2,6},{4,0},{6,2},{8,12},{10,14},{12,8},{14,10},{1,5},{3,7},... | collective-permute-start | bytes 221192 | tf_op jit(solution)/shard_map/ppermute | solution.py:203
  29.6 3.3 %collective-permute-start.11 = (bf16[16,2304]{1,0:T(8,128)(2,1)S(1)}, bf16[16,2304]{1,0:T(8,128)(2,1)S(1)}, u32[]{:S(2)}, u32[]{:S(2)}) collective-permute-start(bf16[16,2304]{1,0:T(8,128)(2,1)S(1)} %get-tuple-element.36), channel_id=1, source_target_pairs={{0,8},{2,10},{4,12},{6,14},{8,0},{10,2},{12,4},{14,6},{1,9},{3,11}... | collective-permute-start | bytes 221192 | tf_op jit(solution)/shard_map/ppermute | solution.py:203
  33.1 2.4 %collective-permute-start.13 = (bf16[16,2304]{1,0:T(8,128)(2,1)S(1)}, bf16[16,2304]{1,0:T(8,128)(2,1)S(1)}, u32[]{:S(2)}, u32[]{:S(2)}) collective-permute-start(bf16[16,2304]{1,0:T(8,128)(2,1)S(1)} %get-tuple-element.38), channel_id=1, source_target_pairs={{0,12},{2,14},{4,8},{6,10},{8,4},{10,6},{12,0},{14,2},{1,13},{3,15... | collective-permute-start | bytes 221192 | tf_op jit(solution)/shard_map/ppermute | solution.py:203
  35.4 2.3 %collective-permute-start.14 = (bf16[16,2304]{1,0:T(8,128)(2,1)S(1)}, bf16[16,2304]{1,0:T(8,128)(2,1)S(1)}, u32[]{:S(2)}, u32[]{:S(2)}) collective-permute-start(bf16[16,2304]{1,0:T(8,128)(2,1)S(1)} %get-tuple-element.39), channel_id=1, source_target_pairs={{0,14},{2,12},{4,10},{6,8},{8,6},{10,4},{12,2},{14,0},{1,15},{3,13... | collective-permute-start | bytes 221192 | tf_op jit(solution)/shard_map/ppermute | solution.py:203
  37.7 1.9 %resident.1.refs_8_ = bf16[4,48,4096]{2,1,0:T(8,128)(2,1)} custom-call(s32[1]{0:T(128)} %bitcast.me_ref, f32[16]{0:T(128)S(1)} %copy-done.5, bf16[2,64,64]{2,1,0:T(8,128)(2,1)S(1)} %get-tuple-element.40.kept, bf16[2,64,4096]{2,1,0:T(8,128)(2,1)S(1)} %copy-done), custom_call_target="tpu_custom_call" | custom-call | flops 67108864 | bytes 2097152 | tf_op jit(solution)/shard_map/resident/pallas_call | solution.py:255
  39.7 1.4 %collective-permute-done.11.refs_4_ = bf16[16,2304]{1,0:T(8,128)(2,1)S(1)} collective-permute-done((bf16[16,2304]{1,0:T(8,128)(2,1)S(1)}, bf16[16,2304]{1,0:T(8,128)(2,1)S(1)}, u32[]{:S(2)}, u32[]{:S(2)}) %collective-permute-start.11) | collective-permute-done | bytes 73760 | tf_op jit(solution)/shard_map/ppermute | solution.py:203
  41.0 2.9 %collective-permute-done.12.refs_5_ = bf16[16,2304]{1,0:T(8,128)(2,1)S(1)} collective-permute-done((bf16[16,2304]{1,0:T(8,128)(2,1)S(1)}, bf16[16,2304]{1,0:T(8,128)(2,1)S(1)}, u32[]{:S(2)}, u32[]{:S(2)}) %collective-permute-start.12) | collective-permute-done | bytes 73760 | tf_op jit(solution)/shard_map/ppermute | solution.py:203
  43.9 2.3 %guest.1 = bf16[4,48,4096]{2,1,0:T(8,128)(2,1)} custom-call(s32[1]{0:T(128)} %bitcast.me_ref, s32[4,3]{1,0:T(4,128)S(1)} %copy-done.3, f32[16]{0:T(128)S(1)} %copy-done.5, bf16[16,2304]{1,0:T(8,128)(2,1)S(1)} %get-tuple-element.32.refs_0_, bf16[16,2304]{1,0:T(8,128)(2,1)S(1)} %collective-permute-done.8.refs_1_, ...), custom_call_target="tpu_custom_call", output_to_operand_aliasing={{}: (11, {})} | custom-call | flops 33554432 | bytes 1048576 | tf_op jit(solution)/shard_map/guest/pallas_call | solution.py:290
  (26 shorter events, 0.7 us)
Async XLA Ops:
  0.0 4.6 %copy-start = (bf16[2,64,4096]{2,1,0:T(8,128)(2,1)S(1)}, bf16[2,64,4096]{2,1,0:T(8,128)(2,1)}, u32[]{:S(2)}) copy-start(bf16[2,64,4096]{2,1,0:T(8,128)(2,1)} %up.3) | copy-start | bytes 3145732
  0.0 1.3 %copy-start.1 = (bf16[4,32,4096]{2,1,0:T(8,128)(2,1)S(1)}, bf16[4,32,4096]{2,1,0:T(8,128)(2,1)}, u32[]{:S(2)}) copy-start(bf16[4,32,4096]{2,1,0:T(8,128)(2,1)} %hidden.1) | copy-start | bytes 3145732
  1.3 1.2 %copy-start.2 = (bf16[2,64,4096]{2,1,0:T(8,128)(2,1)S(1)}, bf16[2,64,4096]{2,1,0:T(8,128)(2,1)}, u32[]{:S(2)}) copy-start(bf16[2,64,4096]{2,1,0:T(8,128)(2,1)} %down.1) | copy-start | bytes 3145732
  2.5 0.7 %copy-start.4 = (f32[4096]{0:T(1024)S(1)}, f32[4096]{0:T(1024)}, u32[]{:S(2)}) copy-start(f32[4096]{0:T(1024)} %param.11) | copy-start | bytes 49156
  3.3 1.3 %copy-start.3 = (s32[4,3]{1,0:T(4,128)S(1)}, s32[4,3]{1,0:T(4,128)}, u32[]{:S(2)}) copy-start(s32[4,3]{1,0:T(4,128)} %moves.7) | copy-start | bytes 148
  3.3 14.4 %copy-start.6 = (s32[16]{0:T(128)S(1)}, s32[16]{0:T(128)}, u32[]{:S(2)}) copy-start(s32[16]{0:T(128)} %lengths.1) | copy-start | bytes 196
  3.3 34.5 %copy-start.5 = (f32[16]{0:T(128)S(1)}, f32[16]{0:T(128)}, u32[]{:S(2)}) copy-start(f32[16]{0:T(128)} %scales.3) | copy-start | bytes 196
  4.1 8.7 %collective-permute-start = (f32[2,64,128]{2,1,0:T(8,128)S(1)}, f32[2,64,128]{2,1,0:T(8,128)S(1)}, u32[]{:S(2)}, u32[]{:S(2)}) collective-permute-start(f32[2,64,128]{2,1,0:T(8,128)S(1)} %project.1.mine), channel_id=1, source_target_pairs={{0,1},{1,0},{2,3},{3,2},{4,5},{5,4},{6,7},{7,6},{8,9},{9,8},{10,11... | collective-permute-start | bytes 196616 | tf_op jit(solution)/shard_map/ppermute | solution.py:245
  5.6 8.4 %collective-permute-start.1 = (bf16[16,2048]{1,0:T(8,128)(2,1)S(1)}, bf16[16,2048]{1,0:T(8,128)(2,1)S(1)}, u32[]{:S(2)}, u32[]{:S(2)}) collective-permute-start(bf16[16,2048]{1,0:T(8,128)(2,1)S(1)} %get-tuple-element.25), channel_id=1, source_target_pairs={{0,2},{2,0},{4,6},{6,4},{8,10},{10,8},{12,14},{14,12},{1,3},{3,1},... | collective-permute-start | bytes 196616 | tf_op jit(solution)/shard_map/ppermute | solution.py:203
  8.2 9.5 %collective-permute-start.2 = (bf16[16,2048]{1,0:T(8,128)(2,1)S(1)}, bf16[16,2048]{1,0:T(8,128)(2,1)S(1)}, u32[]{:S(2)}, u32[]{:S(2)}) collective-permute-start(bf16[16,2048]{1,0:T(8,128)(2,1)S(1)} %get-tuple-element.26), channel_id=1, source_target_pairs={{0,4},{2,6},{4,0},{6,2},{8,12},{10,14},{12,8},{14,10},{1,5},{3,7},... | collective-permute-start | bytes 196616 | tf_op jit(solution)/shard_map/ppermute | solution.py:203
  9.7 8.7 %collective-permute-start.3 = (bf16[16,2048]{1,0:T(8,128)(2,1)S(1)}, bf16[16,2048]{1,0:T(8,128)(2,1)S(1)}, u32[]{:S(2)}, u32[]{:S(2)}) collective-permute-start(bf16[16,2048]{1,0:T(8,128)(2,1)S(1)} %get-tuple-element.27), channel_id=1, source_target_pairs={{0,6},{2,4},{4,2},{6,0},{8,14},{10,12},{12,10},{14,8},{1,7},{3,5},... | collective-permute-start | bytes 196616 | tf_op jit(solution)/shard_map/ppermute | solution.py:203
  9.8 8.7 %collective-permute-start.4 = (bf16[16,2048]{1,0:T(8,128)(2,1)S(1)}, bf16[16,2048]{1,0:T(8,128)(2,1)S(1)}, u32[]{:S(2)}, u32[]{:S(2)}) collective-permute-start(bf16[16,2048]{1,0:T(8,128)(2,1)S(1)} %get-tuple-element.28), channel_id=1, source_target_pairs={{0,8},{2,10},{4,12},{6,14},{8,0},{10,2},{12,4},{14,6},{1,9},{3,11}... | collective-permute-start | bytes 196616 | tf_op jit(solution)/shard_map/ppermute | solution.py:203
  12.8 10.1 %collective-permute-start.5 = (bf16[16,2048]{1,0:T(8,128)(2,1)S(1)}, bf16[16,2048]{1,0:T(8,128)(2,1)S(1)}, u32[]{:S(2)}, u32[]{:S(2)}) collective-permute-start(bf16[16,2048]{1,0:T(8,128)(2,1)S(1)} %get-tuple-element.29), channel_id=1, source_target_pairs={{0,10},{2,8},{4,14},{6,12},{8,2},{10,0},{12,6},{14,4},{1,11},{3,9}... | collective-permute-start | bytes 196616 | tf_op jit(solution)/shard_map/ppermute | solution.py:203
  14.0 8.9 %collective-permute-start.6 = (bf16[16,2048]{1,0:T(8,128)(2,1)S(1)}, bf16[16,2048]{1,0:T(8,128)(2,1)S(1)}, u32[]{:S(2)}, u32[]{:S(2)}) collective-permute-start(bf16[16,2048]{1,0:T(8,128)(2,1)S(1)} %get-tuple-element.30), channel_id=1, source_target_pairs={{0,12},{2,14},{4,8},{6,10},{8,4},{10,6},{12,0},{14,2},{1,13},{3,15... | collective-permute-start | bytes 196616 | tf_op jit(solution)/shard_map/ppermute | solution.py:203
  17.6 7.1 %collective-permute-start.7 = (bf16[16,2048]{1,0:T(8,128)(2,1)S(1)}, bf16[16,2048]{1,0:T(8,128)(2,1)S(1)}, u32[]{:S(2)}, u32[]{:S(2)}) collective-permute-start(bf16[16,2048]{1,0:T(8,128)(2,1)S(1)} %get-tuple-element.31), channel_id=1, source_target_pairs={{0,14},{2,12},{4,10},{6,8},{8,6},{10,4},{12,2},{14,0},{1,15},{3,13... | collective-permute-start | bytes 196616 | tf_op jit(solution)/shard_map/ppermute | solution.py:203
  26.1 7.0 %collective-permute-start.8 = (bf16[16,2304]{1,0:T(8,128)(2,1)S(1)}, bf16[16,2304]{1,0:T(8,128)(2,1)S(1)}, u32[]{:S(2)}, u32[]{:S(2)}) collective-permute-start(bf16[16,2304]{1,0:T(8,128)(2,1)S(1)} %get-tuple-element.33), channel_id=1, source_target_pairs={{0,2},{2,0},{4,6},{6,4},{8,10},{10,8},{12,14},{14,12},{1,3},{3,1},... | collective-permute-start | bytes 221192 | tf_op jit(solution)/shard_map/ppermute | solution.py:203
  26.7 8.7 %collective-permute-start.9 = (bf16[16,2304]{1,0:T(8,128)(2,1)S(1)}, bf16[16,2304]{1,0:T(8,128)(2,1)S(1)}, u32[]{:S(2)}, u32[]{:S(2)}) collective-permute-start(bf16[16,2304]{1,0:T(8,128)(2,1)S(1)} %get-tuple-element.34), channel_id=1, source_target_pairs={{0,4},{2,6},{4,0},{6,2},{8,12},{10,14},{12,8},{14,10},{1,5},{3,7},... | collective-permute-start | bytes 221192 | tf_op jit(solution)/shard_map/ppermute | solution.py:203
  29.1 10.5 %collective-permute-start.10 = (bf16[16,2304]{1,0:T(8,128)(2,1)S(1)}, bf16[16,2304]{1,0:T(8,128)(2,1)S(1)}, u32[]{:S(2)}, u32[]{:S(2)}) collective-permute-start(bf16[16,2304]{1,0:T(8,128)(2,1)S(1)} %get-tuple-element.35), channel_id=1, source_target_pairs={{0,6},{2,4},{4,2},{6,0},{8,14},{10,12},{12,10},{14,8},{1,7},{3,5},... | collective-permute-start | bytes 221192 | tf_op jit(solution)/shard_map/ppermute | solution.py:203
  29.6 11.4 %collective-permute-start.11 = (bf16[16,2304]{1,0:T(8,128)(2,1)S(1)}, bf16[16,2304]{1,0:T(8,128)(2,1)S(1)}, u32[]{:S(2)}, u32[]{:S(2)}) collective-permute-start(bf16[16,2304]{1,0:T(8,128)(2,1)S(1)} %get-tuple-element.36), channel_id=1, source_target_pairs={{0,8},{2,10},{4,12},{6,14},{8,0},{10,2},{12,4},{14,6},{1,9},{3,11}... | collective-permute-start | bytes 221192 | tf_op jit(solution)/shard_map/ppermute | solution.py:203
  33.0 11.0 %collective-permute-start.12 = (bf16[16,2304]{1,0:T(8,128)(2,1)S(1)}, bf16[16,2304]{1,0:T(8,128)(2,1)S(1)}, u32[]{:S(2)}, u32[]{:S(2)}) collective-permute-start(bf16[16,2304]{1,0:T(8,128)(2,1)S(1)} %get-tuple-element.37), channel_id=1, source_target_pairs={{0,10},{2,8},{4,14},{6,12},{8,2},{10,0},{12,6},{14,4},{1,11},{3,9}... | collective-permute-start | bytes 221192 | tf_op jit(solution)/shard_map/ppermute | solution.py:203
  33.1 10.9 %collective-permute-start.13 = (bf16[16,2304]{1,0:T(8,128)(2,1)S(1)}, bf16[16,2304]{1,0:T(8,128)(2,1)S(1)}, u32[]{:S(2)}, u32[]{:S(2)}) collective-permute-start(bf16[16,2304]{1,0:T(8,128)(2,1)S(1)} %get-tuple-element.38), channel_id=1, source_target_pairs={{0,12},{2,14},{4,8},{6,10},{8,4},{10,6},{12,0},{14,2},{1,13},{3,15... | collective-permute-start | bytes 221192 | tf_op jit(solution)/shard_map/ppermute | solution.py:203
  35.4 8.5 %collective-permute-start.14 = (bf16[16,2304]{1,0:T(8,128)(2,1)S(1)}, bf16[16,2304]{1,0:T(8,128)(2,1)S(1)}, u32[]{:S(2)}, u32[]{:S(2)}) collective-permute-start(bf16[16,2304]{1,0:T(8,128)(2,1)S(1)} %get-tuple-element.39), channel_id=1, source_target_pairs={{0,14},{2,12},{4,10},{6,8},{8,6},{10,4},{12,2},{14,0},{1,15},{3,13... | collective-permute-start | bytes 221192 | tf_op jit(solution)/shard_map/ppermute | solution.py:203
